TPU v7x, 32 devices: a whole 2x2x4 slice. The times are simulated.
32 devices in a mesh: dp: 8 (over z, y), seq: 4 (over x, core).
Axes of the slice: x: 2, y: 2, z: 4, core: 2. Of those that a mesh axis runs over, the one named last changes fastest.
Arguments:
- inputs: float32 [512, 64, 768], P('seq', 'dp'), may hold values from -6 to 6
- item_counts: int32 [8], P('dp'), may hold values from 4 to 8, as said below
- lengths: int32 [64], P('dp'), may hold values from 32 to 512, as said below
- gain_one: float32 [768], replicated, may hold values from 0.1 to 1.9
- shift_one: float32 [768], replicated, may hold values from -3 to 3
- weight_in: bfloat16 [768, 3072], replicated, may hold values from -0.21875 to 0.21875
- bias_in: float32 [3072], replicated, may hold values from -3 to 3
- weight_out: bfloat16 [3072, 768], replicated, may hold values from -0.15625 to 0.15625
- bias_out: float32 [768], replicated, may hold values from -3 to 3
- gain_two: float32 [768], replicated, may hold values from 0.1 to 1.9
- shift_two: float32 [768], replicated, may hold values from -3 to 3
- cotangent: float32 [512, 64, 768], P('seq', 'dp'), may hold values from -6 to 6
Outputs:
- layer_out: float32 [512, 64, 768], P('seq', 'dp')
- input_grad: float32 [512, 64, 768], P('seq', 'dp')
- gain_one_grad: float32 [768], replicated
- shift_one_grad: float32 [768], replicated
- weight_in_grad: float32 [768, 3072], replicated
- bias_in_grad: float32 [3072], replicated
- weight_out_grad: float32 [3072, 768], replicated
- bias_out_grad: float32 [768], replicated
- gain_two_grad: float32 [768], replicated
- shift_two_grad: float32 [768], replicated
Inputs may be any that keep to these rules, and one draw needn't show every extreme that they name: `item_counts`: at least one index of dp has all 8 slots in use. `lengths`: slots at or beyond their device's count are empty whatever their length. On every index of dp one slot in use has length 512.
All inputs are finite; a program needn't handle non-finite values.
Results may differ from a plain program's by a relative error of at most 0.0075.
Values may be sent and summed in bfloat16 or wider, within the bound.
A program may use at most 192 MiB of HBM per device.

v0:
```python
import functools
import math

import jax
import jax.numpy as jnp
import numpy as np
from jax import lax
from jax.experimental import pallas as pl
from jax.experimental.pallas import tpu as pltpu
from jax.sharding import PartitionSpec as P

EPSILON = 1e-05
MESH = pl.DeviceIdType.MESH
LANES = 128
WIDE = 512
BF16 = jnp.bfloat16
F32 = jnp.float32


def dft_tables(count):
    index = np.arange(count, dtype=np.int64)
    turns = (index[:, None] * index[None, :] % count).astype(np.float32)
    angle = (turns * np.float32(2.0 * math.pi / count)).astype(np.float64)
    return np.cos(angle).astype(np.float32), np.sin(angle).astype(np.float32)


def aligned(value, step):
    return pl.multiple_of(value, step)


def bit_of(value, k):
    return (value // k) % 2


def flipped(value, k):
    return value + k * (1 - 2 * bit_of(value, k))


def axis_bits(axis, size):
    return [(axis, 1 << b) for b in range(size.bit_length() - 1)]


class Cube:
    def __init__(self, sizes, mids):
        dp, seq = sizes
        bits = axis_bits(1, seq) + axis_bits(0, dp)
        first, near, rest = bits[:1], bits[1:4], bits[4:]
        self.orders = [first + [near[i] for i in mid] + rest for mid in mids]
        self.bits = bits
        self.stages = len(bits)
        self.me = (lax.axis_index("dp"), lax.axis_index("seq"))
        self.values = {bit: self.value(bit) for bit in bits}
        self.partners = {bit: self.partner(bit) for bit in bits}

    def value(self, bit):
        return bit_of(self.me[bit[0]], bit[1])

    def partner(self, bit):
        axis, k = bit
        other = flipped(self.me[axis], k)
        return (other, self.me[1]) if axis == 0 else (self.me[0], other)

    def offset(self, order, level, rows):
        total = 0
        for s in range(level):
            total = total + self.values[self.orders[order][s]] * (rows >> (s + 1))
        return total


class Exchange:
    def __init__(self, size, rows, buf, send, recv):
        self.size, self.rows, self.buf, self.send_sem, self.recv_sem = size, rows, buf, send, recv
        self.dp, self.q = lax.axis_index("dp"), lax.axis_index("seq")
        self.order = [1 << b for b in reversed(range(size.bit_length() - 1))]

    def owner(self, pattern):
        index = self.q
        for k in self.order:
            if pattern & k:
                index = flipped(index, k)
        return index

    def copy(self, slot, pattern):
        hop = pattern & -pattern
        place = pl.ds(aligned(self.owner(pattern - hop) * self.rows, self.rows), self.rows)
        ref = self.buf.at[slot, place]
        return pltpu.make_async_remote_copy(
            src_ref=ref,
            dst_ref=ref,
            send_sem=self.send_sem.at[slot, pattern],
            recv_sem=self.recv_sem.at[slot, pattern],
            device_id=(self.dp, flipped(self.q, hop)),
            device_id_type=MESH,
        )

    def patterns(self, far):
        return range(1, self.size) if far else range(1, 2)

    def start_own(self, slot, far):
        for pattern in self.patterns(far):
            if pattern & (pattern - 1) == 0:
                self.copy(slot, pattern).start()

    def forward(self, slot):
        for pattern in self.patterns(True):
            if pattern & 1 == 0:
                self.copy(slot, pattern).wait_recv()
                for k in self.order:
                    if k < (pattern & -pattern):
                        self.copy(slot, pattern | k).start()

    def wait_near(self, slot, far):
        for pattern in self.patterns(far):
            if pattern & 1:
                self.copy(slot, pattern).wait_recv()

    def wait_sends(self, slot, far):
        for pattern in self.patterns(far):
            self.copy(slot, pattern).wait_send()


def greet(partners):
    barrier = pltpu.get_barrier_semaphore()
    for partner in partners:
        pl.semaphore_signal(barrier, inc=1, device_id=partner, device_id_type=MESH)
    return lambda: pl.semaphore_wait(barrier, len(partners))


def rank_slots(count_ref, length_ref, perm_s, slen_s, slots):
    count = count_ref[0]
    live = [jnp.where(i < count, length_ref[i], 0) for i in range(slots)]
    ranks = []
    for i in range(slots):
        rank = 0
        for k in range(slots):
            if k != i:
                ahead = live[k] >= live[i] if k < i else live[k] > live[i]
                rank = rank + jnp.where(ahead, 1, 0)
        ranks.append(rank)
    for j in range(slots):
        perm, length = 0, 0
        for i in range(slots):
            here = ranks[i] == j
            perm = perm + jnp.where(here, i, 0)
            length = length + jnp.where(here, live[i], 0)
        perm_s[j] = perm
        slen_s[j] = length


def live_rows(slen_s, slot, first, rows):
    position = first + lax.broadcasted_iota(jnp.int32, (rows, 1), 0)
    return position < slen_s[slot]


def fold8(values):
    rows, lanes = values.shape
    return values.reshape(rows // 8, 8, lanes).sum(axis=0)


def normalize(values):
    center = values - jnp.mean(values, axis=-1, keepdims=True)
    spread = jnp.mean(center * center, axis=-1, keepdims=True)
    inverse = lax.rsqrt(spread + EPSILON)
    return center * inverse, inverse


def norm_back(grad_hat, normal, inverse):
    first = jnp.mean(grad_hat, axis=-1, keepdims=True)
    second = jnp.mean(grad_hat * normal, axis=-1, keepdims=True)
    return inverse * (grad_hat - first - normal * second)


def mix_slot(slot, far, exchange, tables, buf, uv, place):
    rows = exchange.rows
    if far:
        table, block = tables[...], buf[slot]
    else:
        base = aligned(exchange.q // 2 * (2 * rows), 2 * rows)
        table, block = tables[:, pl.ds(base, 2 * rows)], buf[slot, pl.ds(base, 2 * rows), :]
    both = jnp.dot(table, block, preferred_element_type=F32).astype(BF16)
    width = both.shape[1]
    uv[pl.ds(place, rows), :width] = both[:rows]
    uv[pl.ds(place, rows), width:] = both[rows:]


def group_at(i, near_groups, count):
    if near_groups == 0:
        return count - 1 - i
    return jnp.where(i < near_groups, count - near_groups + i, count - 1 - i)


def forward_kernel(cfg, *refs):
    sizes, far_slots, slots, group, agrees = cfg
    if agrees:
        choice_o, (mine, theirs, say_sem, hear_sem) = refs[agrees], refs[-4:]
        refs = refs[:agrees] + refs[agrees + 1 : -4]
    vec_refs, refs = refs[2:8], refs[:2] + refs[8:]
    (
        count_ref, length_ref, x_hbm, cot_hbm, wi_hbm, wo_hbm, sc_hbm, hc_hbm,
        act_o, dg_o, nrm_o, sum_o, gs_o, gb_o, lo_o, part_o,
        perm_s, slen_s, x_v, cot_v, wi_v, wo_v, sc_v, hc_v, buf, uv, sum_v, nrm_v, act_v, dg_v, gs_v, gb_v, lo_v, br_v, vec_ref,
        load_sem, out_sem, send_sem, recv_sem,
    ) = refs
    rows, _, features = x_v.shape
    wide = wi_v.shape[1]
    seq_total = rows * sizes[1]
    scale = 1.0 / math.sqrt(features * seq_total)
    exchange = Exchange(sizes[1], rows, buf, send_sem, recv_sem)
    q = exchange.q
    first = q * rows
    gain_one, shift_one, bias_out, gain_two, shift_two = (lambda i=i: vec_ref[i : i + 1, :] for i in range(5))
    loads = [
        pltpu.make_async_copy(x_hbm, x_v, load_sem.at[0]),
        pltpu.make_async_copy(sc_hbm.at[q], sc_v, load_sem.at[1]),
        pltpu.make_async_copy(hc_hbm, hc_v, load_sem.at[2]),
        pltpu.make_async_copy(wi_hbm, wi_v, load_sem.at[3]),
        pltpu.make_async_copy(wo_hbm, wo_v, load_sem.at[4]),
        pltpu.make_async_copy(cot_hbm, cot_v, load_sem.at[5]),
    ]
    loads[0].start()
    partners = [(exchange.dp, flipped(q, k)) for k in exchange.order]
    peers = [(lax.rem(exchange.dp + i, sizes[0]), q) for i in range(1, sizes[0])] if agrees else []
    met = greet(partners + peers)
    row = 0
    for vec in vec_refs:
        for i in range(vec.shape[0] // features):
            vec_ref[row : row + 1, :] = vec[pl.ds(i * features, features)].reshape(1, features)
            row += 1
    rank_slots(count_ref, length_ref, perm_s, slen_s, slots)
    for load in loads[1:3]:
        load.start()
    loads[0].wait()
    loads[3].start()
    met()

    def word(i):
        return pltpu.make_async_remote_copy(
            src_ref=mine,
            dst_ref=theirs.at[i],
            send_sem=say_sem.at[i],
            recv_sem=hear_sem.at[i],
            device_id=peers[i - 1],
            device_id_type=MESH,
        )

    if agrees:
        long = 0
        for i in range(slots):
            long = long + jnp.where((i < count_ref[0]) & (length_ref[i] > 2 * rows), 1, 0)
        mine[...] = jnp.full(mine.shape, long, jnp.int32).astype(F32)
        theirs[0] = mine[...]
        for i in range(1, sizes[0]):
            word(i).start()

    def prepare(i, _):
        slot = jnp.where(i < slots - far_slots, far_slots + i, slots - 1 - i)
        value = jnp.where(live_rows(slen_s, slot, first, rows), x_v[:, perm_s[slot], :], 0.0)
        buf[slot, pl.ds(aligned(first, rows), rows), :] = value.astype(BF16)
        pl.when(slot < far_slots)(lambda: exchange.start_own(slot, True))
        if far_slots < slots:
            pl.when(slot >= far_slots)(lambda: exchange.start_own(slot, False))
        return 0

    lax.fori_loop(0, slots, prepare, 0)
    part_o[...] = jnp.zeros_like(part_o)
    for load in loads[1:3]:
        load.wait()

    batch = group * rows
    span = features
    count = slots // group
    near_groups = (slots - far_slots) // group

    def outs(base):
        place = pl.ds(base, batch)
        early = [
            pltpu.make_async_copy(nrm_v.at[place], nrm_o.at[place], out_sem.at[0]),
            pltpu.make_async_copy(sum_v.at[place], sum_o.at[place], out_sem.at[1]),
        ]
        for n in range(wide // WIDE):
            cut = pl.ds(n * WIDE, WIDE)
            early.append(pltpu.make_async_copy(act_v.at[place, cut], act_o.at[n, place], out_sem.at[4]))
            early.append(pltpu.make_async_copy(dg_v.at[place, cut], dg_o.at[n, place], out_sem.at[5]))
        late = [
            pltpu.make_async_copy(gs_v.at[place], gs_o.at[place], out_sem.at[2]),
            pltpu.make_async_copy(lo_v.at[place], lo_o.at[place], out_sem.at[3]),
            pltpu.make_async_copy(gb_v.at[place], gb_o.at[place], out_sem.at[6]),
        ]
        return early, late

    def bring(slot0):
        for k in reversed(range(group)):
            exchange.forward(slot0 + k)

    def mixing(slot0, far):
        for k in reversed(range(group)):
            exchange.wait_near(slot0 + k, far)
            mix_slot(slot0 + k, far, exchange, sc_v, buf, uv, k * rows)

    def work(i, _):
        slot0 = group_at(i, near_groups, count) * group
        base = aligned(slot0 * rows, batch)
        place = pl.ds(base, batch)
        if near_groups < count:
            pl.when(i >= near_groups)(lambda: mixing(slot0, True))
        if near_groups > 0:
            pl.when(i < near_groups)(lambda: mixing(slot0, False))
        br_v[...] = jnp.dot(uv[...], hc_v[...], preferred_element_type=F32)

        def norm_one(k, _):
            here = pl.ds(aligned(base + k * rows, rows), rows)
            mixed = (br_v[pl.ds(aligned(k * rows, rows), rows), :] * scale).astype(BF16).astype(F32)
            live = live_rows(slen_s, slot0 + k, first, rows)
            total = jnp.where(live, x_v[:, perm_s[slot0 + k], :], 0.0) + mixed
            sum_v[here, :] = total
            hat, _ = normalize(total)
            nrm_v[here, :] = (hat * gain_one() + shift_one()).astype(BF16)
            return 0

        lax.fori_loop(0, group, norm_one, 0)

        @pl.when(i == 0)
        def _():
            loads[3].wait()
            for load in loads[4:]:
                load.start()

        def expand(n, _):
            cut = pl.ds(aligned(n * span, span), span)
            hidden = jnp.dot(nrm_v[place, :], wi_v[:, cut], preferred_element_type=F32) + vec_ref[pl.ds(5 + n, 1), :]
            gate = 0.5 + 0.5 * lax.erf(hidden * math.sqrt(0.5))
            slope = gate + hidden * (jnp.exp(hidden * hidden * -0.5) * (1.0 / math.sqrt(2.0 * math.pi)))
            act_v[place, cut] = (hidden * gate).astype(BF16)
            dg_v[place, cut] = slope.astype(BF16)
            return 0

        lax.fori_loop(0, wide // span, expand, 0)
        for copy in outs(base)[0]:
            copy.start()
        if near_groups < count:

            @pl.when((i + 1 >= near_groups) & (i + 1 < count))
            def _():
                bring(group_at(i + 1, near_groups, count) * group)

        pl.when(i == 0)(loads[4].wait)
        br_v[...] = jnp.dot(act_v[place, :], wo_v[...], preferred_element_type=F32)

        def norm_two(k, _):
            here = pl.ds(aligned(base + k * rows, rows), rows)
            local = pl.ds(aligned(k * rows, rows), rows)
            slot = slot0 + k
            live = live_rows(slen_s, slot, first, rows)
            hat, inverse = normalize(sum_v[here, :] + (br_v[local, :] + bias_out()))
            grad = jnp.where(live, cot_v[:, perm_s[slot], :], 0.0)
            lo_v[here, :] = jnp.where(live, hat * gain_two() + shift_two(), 0.0).astype(BF16)
            part_o[0:8, :] = part_o[0:8, :] + fold8(grad * hat)
            part_o[8:16, :] = part_o[8:16, :] + fold8(grad)
            second = norm_back(grad * gain_two(), hat, inverse)
            low = second.astype(BF16)
            gs_v[here, :] = second
            gb_v[here, :] = low
            part_o[16:24, :] = part_o[16:24, :] + fold8(low.astype(F32))
            return 0

        pl.when(i == 0)(loads[5].wait)
        lax.fori_loop(0, group, norm_two, 0)
        for copy in outs(base)[1]:
            copy.start()
        return 0

    if near_groups == 0:
        bring((count - 1) * group)
    lax.fori_loop(0, count, work, 0)

    def finish(slot, _):
        pl.when(slot < far_slots)(lambda: exchange.wait_sends(slot, True))
        if far_slots < slots:
            pl.when(slot >= far_slots)(lambda: exchange.wait_sends(slot, False))
        return 0

    lax.fori_loop(0, slots, finish, 0)

    if agrees:
        for i in range(1, sizes[0]):
            word(i).wait()
        choice_o[0] = jnp.where(jnp.max(theirs[...]) > far_slots, 1, 0)

    def flush(g, _):
        for copies in outs(aligned(g * batch, batch)):
            for copy in copies:
                copy.wait()
        return 0

    lax.fori_loop(0, count, flush, 0)


def backward_kernel(cfg, *refs):
    sizes, far_slots, slots, group, parts, mids, lags, plan = cfg
    cube = Cube(sizes, mids)
    S = cube.stages
    (
        count_ref, length_ref, gain_ref, part_ref,
        act_hbm, dg_hbm, nrm_hbm, sum_hbm, gs_hbm, gb_hbm, wi_hbm, wo_hbm, sc_hbm, hc_hbm,
        full_o, ig_o, small_o,
        perm_s, slen_s, gs_v, sum_v, nrm_v, gb_v, gh_v, gn_v, act_v, dg_v, wi_v, wo_v, sc_v, hc_v, buf, uv, mix_v, ig_v,
        bin_v, one_v, small_v, gain_v, part_v, full,
    ) = refs[:41]
    landed = refs[41 : 41 + S]
    (
        small_recv, load_sem, sum_sem, stream_sem, out_sem, ig_sem, send_sem, recv_sem,
        rs_s, rs_r, ag_s, ag_r, sm_s, sm_r,
    ) = refs[41 + S :]
    ticks, tick_rows, _ = part_v.shape
    message = tick_rows // parts
    chunks = act_hbm.shape[0]
    per_tick = chunks // ticks
    features = nrm_v.shape[1]
    rows = gs_v.shape[0] // slots
    batch = group * rows
    scale = 1.0 / math.sqrt(features * rows * sizes[1])
    exchange = Exchange(sizes[1], rows, buf, send_sem, recv_sem)
    q = exchange.q
    first = q * rows
    loads = [
        pltpu.make_async_copy(gb_hbm, gb_v, load_sem.at[0]),
        pltpu.make_async_copy(nrm_hbm, nrm_v, load_sem.at[1]),
        pltpu.make_async_copy(gs_hbm, gs_v, load_sem.at[2]),
        pltpu.make_async_copy(sc_hbm.at[q], sc_v, load_sem.at[3]),
        pltpu.make_async_copy(hc_hbm, hc_v, load_sem.at[4]),
    ]

    def turn(i):
        return jnp.where(i < far_slots, far_slots - 1 - i, i) if far_slots < slots else slots - 1 - i

    def sum_copy(i):
        place = pl.ds(aligned(turn(i) * rows, rows), rows)
        return pltpu.make_async_copy(sum_hbm.at[place], sum_v.at[lax.rem(i, 2)], sum_sem.at[lax.rem(i, 2)])

    def streams(n, slot):
        cut = pl.ds(aligned(n * WIDE, WIDE), WIDE)
        return [
            pltpu.make_async_copy(act_hbm.at[n], act_v.at[slot], stream_sem.at[0, slot]),
            pltpu.make_async_copy(wo_hbm.at[cut], wo_v.at[slot], stream_sem.at[1, slot]),
            pltpu.make_async_copy(dg_hbm.at[n], dg_v.at[slot], stream_sem.at[2, slot]),
            pltpu.make_async_copy(wi_hbm.at[:, cut], wi_v.at[slot], stream_sem.at[3, slot]),
        ]

    loads[0].start()
    streams(0, 0)[0].start()
    met = greet([cube.partner(bit) for bit in cube.bits])
    rank_slots(count_ref, length_ref, perm_s, slen_s, slots)

    starts = [[j * message + cube.offset(j, level, message) for level in range(S + 1)] for j in range(parts)]

    def rs(m, t, j, s):
        bit = cube.orders[j][s]
        half = message >> (s + 1)
        off = starts[j][s] + (1 - cube.values[bit]) * half
        return pltpu.make_async_remote_copy(
            src_ref=part_v.at[t, pl.ds(aligned(off, 16), half)],
            dst_ref=landed[s].at[m],
            send_sem=rs_s.at[s],
            recv_sem=rs_r.at[s, m],
            device_id=cube.partners[bit],
            device_id_type=MESH,
        )

    def ag(m, t, j, s):
        bit = cube.orders[j][s]
        half = message >> (s + 1)
        ref = full.at[t, pl.ds(aligned(starts[j][s + 1], 16), half)]
        return pltpu.make_async_remote_copy(
            src_ref=ref,
            dst_ref=ref,
            send_sem=ag_s.at[s],
            recv_sem=ag_r.at[s, m],
            device_id=cube.partners[bit],
            device_id_type=MESH,
        )

    def add(m, t, j, s):
        half = message >> (s + 1)
        place = pl.ds(aligned(starts[j][s + 1], 16), half)
        total = part_v[t, place, :].astype(F32) + landed[s][m].astype(F32)
        target = full if s == S - 1 else part_v
        target[t, place, :] = total.astype(BF16)

    def out(t, j):
        place = pl.ds(j * message, message)
        return pltpu.make_async_copy(full.at[t, place], full_o.at[t, place], out_sem.at[t, j])

    def event(k, m, t, j):
        if k == 0:
            rs(m, t, j, 0).start()
        elif k <= S:
            rs(m, t, j, k - 1).wait_recv()
            add(m, t, j, k - 1)
            (rs(m, t, j, k) if k < S else ag(m, t, j, S - 1)).start()
        elif k < 2 * S:
            s = 2 * S - k
            ag(m, t, j, s).wait_recv()
            ag(m, t, j, s - 1).start()
        else:
            ag(m, t, j, 0).wait_recv()
            out(t, j).start()

    def sends_done():
        for s in range(S):
            for sem in (rs_s.at[s], ag_s.at[s]):
                pltpu.make_async_copy(landed[s], landed[s], sem).wait()

    when = [0 if per_tick == 1 and parts == 4 else parts]
    for lag in lags:
        when.append(when[-1] + lag)

    def events(tick, j):
        for k in reversed(range(2 * S + 1)):
            t = tick + (j - when[k]) // parts
            jj = (j - when[k]) % parts
            pl.when((t >= 0) & (t < ticks))(functools.partial(event, k, t * parts + jj, t, jj))

    bin_v[...] = jnp.zeros_like(bin_v)
    one_v[...] = jnp.zeros_like(one_v)
    gain_v[...] = gain_ref[...].reshape(1, features)
    gn_v[...] = jnp.zeros_like(gn_v)
    small_v[...] = jnp.zeros_like(small_v)
    loads[0].wait()
    for copy in streams(0, 0)[1:]:
        copy.start()
    loads[1].start()
    met()

    def load_rest():
        for load in loads[2:]:
            load.start()
        for i in range(2):
            sum_copy(i).start()


    def contract(left, right, dims):
        return lax.dot_general(left, right, ((dims, dims), ((), ())), preferred_element_type=F32)

    def weigh_out(n, slot, t, base):
        streams(n, slot)[0].wait()
        grad = contract(act_v[slot], gb_v[...], (0,)).astype(BF16)
        for i in range(features // LANES):
            part_v[t, pl.ds(base + i * WIDE, WIDE), :] = grad[:, i * LANES : (i + 1) * LANES]

    def pull(n, slot, t, base):
        streams(n, slot)[1].wait()
        streams(n, slot)[2].wait()
        pulled = contract(gb_v[...], wo_v[slot], (1,)) * dg_v[slot].astype(F32)
        pulled = pulled.astype(BF16)
        gh_v[...] = pulled
        bin_v[n] = fold8(pulled.astype(F32))

    def weigh_in(n, slot, t, base):
        pl.when(n == 0)(loads[1].wait)
        grad = contract(nrm_v[...], gh_v[...], (0,)).astype(BF16)
        for i in range(WIDE // LANES):
            place = pl.ds(base + features // LANES * WIDE + i * features, features)
            part_v[t, place, :] = grad[:, i * LANES : (i + 1) * LANES]

    def spread(n, slot, t, base):
        streams(n, slot)[3].wait()
        for i in range(2):
            here = pl.ds(i * (slots // 2) * rows, slots // 2 * rows)
            gn_v[here, :] = gn_v[here, :] + contract(gh_v[here, :], wi_v[slot], (1,))

    steps = [weigh_out, pull, weigh_in, spread]

    def compute(tick, j):
        if per_tick == 1 and parts == 4:
            slot = lax.rem(tick, 2)
            if j == 0:
                for copy in streams(tick + 1, 1 - slot):
                    pl.when(tick + 1 < chunks)(copy.start)
            steps[j](tick, slot, tick, 0)
        elif j == 0:

            def whole(u, _):
                n = tick * per_tick + u
                slot = lax.rem(n, 2)
                for copy in streams(n + 1, 1 - slot):
                    pl.when(n + 1 < chunks)(copy.start)
                for step in steps:
                    step(n, slot, tick, aligned(u * (tick_rows // per_tick), LANES))
                return 0

            lax.fori_loop(0, per_tick, whole, 0)

    def back(i, _):
        slot = turn(i)
        here = pl.ds(aligned(slot * rows, rows), rows)
        pl.when(i == 0)(loads[2].wait)
        sum_copy(i).wait()
        hat, inverse = normalize(sum_v[lax.rem(i, 2)])
        grad = gn_v[here, :]
        one_v[0:8, :] = one_v[0:8, :] + fold8(grad * hat)
        one_v[8:16, :] = one_v[8:16, :] + fold8(grad)
        grad = gs_v[here, :] + norm_back(grad * gain_v[...], hat, inverse)
        gs_v[here, :] = grad
        buf[slot, pl.ds(aligned(first, rows), rows), :] = grad.astype(BF16)
        pl.when(i < far_slots)(lambda: exchange.start_own(slot, True))
        if far_slots < slots:
            pl.when(i >= far_slots)(lambda: exchange.start_own(slot, False))
        pl.when(i + 2 < slots)(lambda: sum_copy(i + 2).start())
        return 0

    def small_copy(s):
        return pltpu.make_async_remote_copy(
            src_ref=small_v.at[s],
            dst_ref=small_recv.at[s],
            send_sem=sm_s.at[s],
            recv_sem=sm_r.at[s],
            device_id=cube.partners[cube.bits[s]],
            device_id_type=MESH,
        )

    def small_start():
        row = 0
        vectors = [one_v[0:8, :], one_v[8:16, :]] + [bin_v[n] for n in range(chunks)]
        vectors += [part_ref[16:24, :], part_ref[0:8, :], part_ref[8:16, :]]
        for vector in vectors:
            vector = jnp.sum(vector, axis=0, keepdims=True)
            for i in range(vector.shape[1] // LANES):
                small_v[0, row : row + 1, :] = vector[:, i * LANES : (i + 1) * LANES]
                row += 1
        small_copy(0).start()

    def small_step(s):
        small_copy(s).wait()
        if s + 1 < S:
            small_v[s + 1] = small_v[s] + small_recv[s]
            small_copy(s + 1).start()
        else:
            small_o[...] = small_v[s] + small_recv[s]

    count = slots // group
    near_groups = (slots - far_slots) // group

    def grad_copy(i):
        base = aligned(group_at(i, near_groups, count) * batch, batch)
        return pltpu.make_async_copy(ig_v.at[lax.rem(i, 2)], ig_o.at[pl.ds(base, batch)], ig_sem.at[lax.rem(i, 2)])

    def mixing(i, k, far):
        slot = group_at(i, near_groups, count) * group + k
        exchange.wait_near(slot, far)
        mix_slot(slot, far, exchange, sc_v, buf, uv, k * rows)

    def hidden_mix(i):
        pl.when(i >= 2)(lambda: grad_copy(i - 2).wait())
        mix_v[...] = jnp.dot(uv[...], hc_v[...], preferred_element_type=F32)

    def finish(i):
        for k in range(group):
            slot = group_at(i, near_groups, count) * group + k
            here = pl.ds(aligned(slot * rows, rows), rows)
            local = pl.ds(k * rows, rows)
            grad = gs_v[here, :] + mix_v[local, :] * scale
            grad = jnp.where(live_rows(slen_s, slot, first, rows), grad, 0.0)
            ig_v[lax.rem(i, 2), local, :] = grad.astype(BF16)
        grad_copy(i).start()

    def bring(i):
        for k in reversed(range(group)):
            exchange.forward(group_at(i, near_groups, count) * group + k)

    small_at, near_at, far_at, lead = plan

    def drain(tick, j):
        d = tick - ticks

        @pl.when(d == 0)
        def _():
            share = -(-slots // parts)
            lax.fori_loop(min(j * share, slots), min((j + 1) * share, slots), back, 0)

        here = lambda at: pl.when(d * parts + j == at)
        if j == small_at % parts:
            here(small_at)(small_start)
        for s in range(S):
            at = small_at + 3 * (s + 1)
            if j == at % parts:
                here(at)(functools.partial(small_step, s))
        if j == 0:

            @pl.when(d == 1)
            def _():
                for load in loads[3:]:
                    load.wait()

        for far, start, low, high in ((False, near_at, 0, near_groups), (True, far_at, near_groups, count)):
            if low == high:
                continue
            i = d - start + low

            @pl.when((i >= low) & (i < high))
            def _():
                subs = [
                    lambda: mixing(i, 0, far),
                    lambda: [mixing(i, k, far) for k in range(1, group)],
                    lambda: hidden_mix(i),
                    lambda: finish(i),
                ]
                for at, sub in enumerate(subs):
                    if min(at, parts - 1) == j:
                        sub()

            if far and j == parts - 1:
                ahead = i + lead
                pl.when((ahead >= low) & (ahead < high))(lambda: bring(ahead))

    last = ticks + max(
        -(-(when[-1] + 1) // parts),
        (small_at + 3 * S) // parts + 1,
        near_at + near_groups,
        far_at + count - near_groups,
    )

    def body(tick, _):
        pl.when(tick == 1)(load_rest)
        for j in range(parts):
            pl.when(tick < ticks)(lambda: compute(tick, j))
            events(tick, j)
            pl.when(tick >= ticks)(lambda: drain(tick, j))
        return 0

    lax.fori_loop(0, last, body, 0)

    def settle(slot, _):
        pl.when(slot < far_slots)(lambda: exchange.wait_sends(slot, True))
        if far_slots < slots:
            pl.when(slot >= far_slots)(lambda: exchange.wait_sends(slot, False))
        return 0

    lax.fori_loop(0, slots, settle, 0)
    for i in range(max(0, count - 2), count):
        grad_copy(i).wait()

    def finish_out(t, _):
        for j in range(parts):
            out(t, j).wait()
        return 0

    lax.fori_loop(0, ticks, finish_out, 0)
    sends_done()


def output_kernel(slots, cuts, places, count_ref, length_ref, full_ref, lo_ref, ig_ref, small_ref, *refs):
    wi_ref, wo_ref, lo_out, ig_out = refs[:4]
    vector_refs, (perm_s, slen_s) = refs[4:-2], refs[-2:]
    step = pl.program_id(0)
    features = wi_ref.shape[0]
    for u in range(full_ref.shape[0]):
        base = u * WIDE
        for i in range(features // LANES):
            wo_ref[base : base + WIDE, i * LANES : (i + 1) * LANES] = full_ref[u, pl.ds(i * WIDE, WIDE), :].astype(F32)
        for i in range(WIDE // LANES):
            start = features // LANES * WIDE + i * features
            wi_ref[:, base + i * LANES : base + (i + 1) * LANES] = full_ref[u, pl.ds(start, features), :].astype(F32)

    @pl.when(step == 0)
    def _():
        rank_slots(count_ref, length_ref, perm_s, slen_s, slots)
        for ref, start in zip(vector_refs, cuts):
            ref[...] = small_ref[start : start + ref.shape[0], :]

    @pl.when(step < places)
    def _():
        for j in range(slots):
            lo_out[:, perm_s[j], :] = lo_ref[j].astype(F32)
            ig_out[:, perm_s[j], :] = ig_ref[j].astype(F32)


ANY = pl.BlockSpec(memory_space=pl.ANY)
SMEM = pl.BlockSpec(memory_space=pltpu.SMEM)
VMEM = pl.BlockSpec(memory_space=pltpu.VMEM)
DMA = pltpu.SemaphoreType.DMA
LAGS = [3, 5, 4, 3, 3, 3, 3, 4, 6, 3]
PLAN = (4, 1, 4, 1)
FAR_PLAN = (4, 1, 4, 1)
MIDS = ((0, 1, 2), (1, 0, 2), (2, 0, 1), (1, 2, 0))
FAR_MIDS = ((1, 2, 0), (2, 1, 0), (1, 0, 2), (2, 0, 1))


def run_forward(sizes, far_slots, slots, *operands, agrees=False, group=2, name="forward", cid=1):
    rows, _, features = operands[8].shape
    wide = operands[10].shape[1]
    seq_total = rows * sizes[1]
    flat, batch, chunks = rows * slots, group * rows, wide // WIDE
    shape = jax.ShapeDtypeStruct
    return pl.pallas_call(
        functools.partial(forward_kernel, (sizes, far_slots, slots, group, len(operands) + 8 if agrees else 0)),
        name=name,
        out_shape=(
            shape((chunks, flat, WIDE), BF16),
            shape((chunks, flat, WIDE), BF16),
            shape((flat, features), BF16),
            shape((flat, features), F32),
            shape((flat, features), F32),
            shape((flat, features), BF16),
            shape((flat, features), BF16),
            shape((24, features), F32),
        )
        + ((shape((1,), jnp.int32),) if agrees else ()),
        in_specs=[SMEM] * 2 + [VMEM] * 6 + [ANY] * 6,
        out_specs=[ANY] * 7 + [VMEM] + [SMEM] * agrees,
        scratch_shapes=[
            pltpu.SMEM((slots,), jnp.int32),
            pltpu.SMEM((slots,), jnp.int32),
            pltpu.VMEM((rows, slots, features), F32),
            pltpu.VMEM((rows, slots, features), F32),
            pltpu.VMEM((features, wide), BF16),
            pltpu.VMEM((wide, features), BF16),
            pltpu.VMEM((2 * rows, seq_total), BF16),
            pltpu.VMEM((2 * features, features), BF16),
            pltpu.VMEM((slots, seq_total, features), BF16),
            pltpu.VMEM((batch, 2 * features), BF16),
            pltpu.VMEM((flat, features), F32),
            pltpu.VMEM((flat, features), BF16),
            pltpu.VMEM((flat, wide), BF16),
            pltpu.VMEM((flat, wide), BF16),
            pltpu.VMEM((flat, features), F32),
            pltpu.VMEM((flat, features), BF16),
            pltpu.VMEM((flat, features), BF16),
            pltpu.VMEM((batch, features), F32),
            pltpu.VMEM((5 + wide // features, features), F32),
            DMA((6,)),
            DMA((7,)),
            DMA((slots, sizes[1])),
            DMA((slots, sizes[1])),
        ]
        + agrees * [pltpu.VMEM((8, LANES), F32), pltpu.VMEM((sizes[0], 8, LANES), F32), DMA((sizes[0],)), DMA((sizes[0],))],
        compiler_params=pltpu.CompilerParams(collective_id=cid, has_side_effects=True, vmem_limit_bytes=62 << 20),
    )(*operands)


def run_backward(sizes, far_slots, slots, ticks, tick_rows, parts, *operands, group=2, mids=None, lags=None, plan=None, name="backward", cid=2):
    devices = sizes[0] * sizes[1]
    chunks, flat, _ = operands[4].shape
    features, wide = operands[10].shape
    rows = flat // slots
    seq_total = rows * sizes[1]
    batch = group * rows
    message = tick_rows // parts
    shape = jax.ShapeDtypeStruct
    mostly_far = far_slots > slots * 5 // 8
    mids = mids or (FAR_MIDS if mostly_far else MIDS)
    plan = plan or (FAR_PLAN if mostly_far else PLAN)
    lags = lags or LAGS
    stages = devices.bit_length() - 1
    lags = (lags[:stages] + [2] * stages)[:stages] + ([2] * stages + lags[-stages:])[-stages:]
    return pl.pallas_call(
        functools.partial(backward_kernel, (sizes, far_slots, slots, group, parts, mids, lags, plan)),
        name=name,
        out_shape=(
            shape((ticks, tick_rows, LANES), BF16),
            shape((flat, features), BF16),
            shape((64, LANES), F32),
        ),
        in_specs=[SMEM] * 2 + [VMEM] * 2 + [ANY] * 10,
        out_specs=[ANY] * 2 + [VMEM],
        scratch_shapes=[
            pltpu.SMEM((slots,), jnp.int32),
            pltpu.SMEM((slots,), jnp.int32),
            pltpu.VMEM((flat, features), F32),
            pltpu.VMEM((2, rows, features), F32),
            pltpu.VMEM((flat, features), BF16),
            pltpu.VMEM((flat, features), BF16),
            pltpu.VMEM((flat, WIDE), BF16),
            pltpu.VMEM((flat, features), F32),
            pltpu.VMEM((2, flat, WIDE), BF16),
            pltpu.VMEM((2, flat, WIDE), BF16),
            pltpu.VMEM((2, features, WIDE), BF16),
            pltpu.VMEM((2, WIDE, features), BF16),
            pltpu.VMEM((2 * rows, seq_total), BF16),
            pltpu.VMEM((2 * features, features), BF16),
            pltpu.VMEM((slots, seq_total, features), BF16),
            pltpu.VMEM((batch, 2 * features), BF16),
            pltpu.VMEM((batch, features), F32),
            pltpu.VMEM((2, batch, features), BF16),
            pltpu.VMEM((chunks, 8, WIDE), F32),
            pltpu.VMEM((16, features), F32),
            pltpu.VMEM((stages, 64, LANES), F32),
            pltpu.VMEM((1, features), F32),
            pltpu.VMEM((ticks, tick_rows, LANES), BF16),
            pltpu.VMEM((ticks, tick_rows, LANES), BF16),
        ]
        + [pltpu.VMEM((ticks * parts, message >> (s + 1), LANES), BF16) for s in range(stages)]
        + [
            pltpu.VMEM((stages, 64, LANES), F32),
            DMA((5,)),
            DMA((2,)),
            DMA((4, 2)),
            DMA((ticks, parts)),
            DMA((2,)),
            DMA((slots, sizes[1])),
            DMA((slots, sizes[1])),
            DMA((stages,)),
            DMA((stages, ticks * parts)),
            DMA((stages,)),
            DMA((stages, ticks * parts)),
            DMA((stages,)),
            DMA((stages,)),
        ],
        compiler_params=pltpu.CompilerParams(collective_id=cid, has_side_effects=True, vmem_limit_bytes=62 << 20),
    )(*operands)


def cut_messages(devices, chunks, chunk_rows):
    per_tick, parts = min(
        (count, -cut)
        for count in range(1, chunks + 1)
        for cut in range(1, 5)
        if chunks % count == 0 and chunk_rows * count % (devices * 16 * cut) == 0
    )
    return per_tick, -parts


def rest_of_layer(far_slots, sizes, cid, known, inputs, item_counts, lengths, vectors, weight_in, weight_out, cotangent, seq_table, hid_table):
    rows, slots, features = inputs.shape
    wide = weight_in.shape[1]
    chunks = wide // WIDE
    chunk_rows = 2 * features * WIDE // LANES
    shape = jax.ShapeDtypeStruct
    per_tick, parts = cut_messages(sizes[0] * sizes[1], chunks, chunk_rows)
    act, dg, nrm, summed, second, low, lo, part = known or run_forward(
        sizes, far_slots, slots,
        item_counts, lengths, *vectors, inputs, cotangent, weight_in, weight_out, seq_table, hid_table,
        cid=cid,
    )
    full, grad, small = run_backward(
        sizes, far_slots, slots, chunks // per_tick, chunk_rows * per_tick, parts,
        item_counts, lengths, vectors[0], part, act, dg, nrm, summed, second, low, weight_in, weight_out, seq_table, hid_table,
        cid=cid + 1,
    )
    side = 2 if chunks % 2 == 0 else 1
    places = 1 << min((chunks // side).bit_length() - 1, 3)
    step = rows // places
    lo, grad = lo.reshape(slots, rows, features), grad.reshape(slots, rows, features)
    heights = [size // LANES for size in (features, features, wide, features, features, features)]
    cuts = [sum(heights[:i]) for i in range(len(heights))]
    slot_first = pl.BlockSpec((slots, step, features), lambda n: (0, jnp.minimum(n, places - 1), 0))
    place_first = pl.BlockSpec((step, slots, features), lambda n: (jnp.minimum(n, places - 1), 0, 0))
    wi_grad, wo_grad, layer_out, input_grad, *vectors = pl.pallas_call(
        functools.partial(output_kernel, slots, cuts, places),
        name="output",
        grid=(chunks // side,),
        out_shape=(
            shape((features, wide), F32),
            shape((wide, features), F32),
            shape(inputs.shape, F32),
            shape(inputs.shape, F32),
            *(shape((height, LANES), F32) for height in heights),
        ),
        in_specs=[SMEM] * 2 + [pl.BlockSpec((side, chunk_rows, LANES), lambda n: (n, 0, 0))] + [slot_first] * 2 + [VMEM],
        out_specs=(
            pl.BlockSpec((features, side * WIDE), lambda n: (0, n)),
            pl.BlockSpec((side * WIDE, features), lambda n: (n, 0)),
            place_first,
            place_first,
            *([VMEM] * len(heights)),
        ),
        scratch_shapes=[pltpu.SMEM((slots,), jnp.int32), pltpu.SMEM((slots,), jnp.int32)],
        compiler_params=pltpu.CompilerParams(vmem_limit_bytes=60 << 20),
    )(item_counts, lengths, full.reshape(chunks, chunk_rows, LANES), lo, grad, small)
    gain_one_grad, shift_one_grad, bias_in_grad, bias_out_grad, gain_two_grad, shift_two_grad = [v.reshape(-1) for v in vectors]
    return (
        layer_out, input_grad, gain_one_grad, shift_one_grad, wi_grad, bias_in_grad, wo_grad, bias_out_grad, gain_two_grad, shift_two_grad,
    )


def per_device(
    inputs, item_counts, lengths, gain_one, shift_one, weight_in, bias_in, weight_out, bias_out, gain_two, shift_two, cotangent
):
    rows, slots, features = inputs.shape
    wide = weight_in.shape[1]
    sizes = (lax.axis_size("dp"), lax.axis_size("seq"))
    seq_total = rows * sizes[1]
    chunks = wide // WIDE
    chunk_rows = 2 * features * WIDE // LANES
    shape = jax.ShapeDtypeStruct

    seq_cos, seq_sin = dft_tables(seq_total)
    hid_cos, hid_sin = dft_tables(features)
    seq_table = [table.reshape(sizes[1], rows, seq_total) for table in (seq_cos, seq_sin)]
    seq_table = jnp.asarray(np.concatenate(seq_table, axis=1).astype(jnp.bfloat16))
    hid_table = jnp.asarray(np.concatenate([hid_cos, -hid_sin], axis=0).astype(jnp.bfloat16))
    vectors = (gain_one, shift_one, bias_out, gain_two, shift_two, bias_in)
    operands = (inputs, item_counts, lengths, vectors, weight_in, weight_out, cotangent, seq_table, hid_table)

    few = slots // 2
    *known, choice = run_forward(
        sizes, few, slots,
        item_counts, lengths, *vectors, inputs, cotangent, weight_in, weight_out, seq_table, hid_table,
        agrees=True, cid=1,
    )
    return lax.cond(
        choice[0] == 0,
        lambda known, *given: rest_of_layer(few, sizes, 2, known, *given),
        lambda known, *given: rest_of_layer(slots, sizes, 4, None, *given),
        tuple(known), *operands,
    )


def solution(mesh):
    placed = (
        P("seq", "dp", None), P("dp"), P("dp"), P(), P(), P(), P(), P(), P(), P(), P(), P("seq", "dp", None),
    )
    wide = P("seq", "dp", None)
    return jax.shard_map(
        per_device,
        mesh=mesh,
        in_specs=placed,
        out_specs=(wide, wide, P(), P(), P(), P(), P(), P(), P(), P()),
        check_vma=False,
    )
```

profile of v0, /device:TPU:0, one launch (start us, length us, event | category | flops | bytes accessed | tf_op | source)
XLA Modules:
  0.0 157.0 jit_solution(8718545280374226165)
XLA Ops:
  1.3 0.0 copy-start
  1.3 0.0 copy-start.1
  1.3 0.0 copy-start.2
  1.3 0.0 copy-start.3
  1.3 0.0 copy-start.4
  1.3 0.0 copy-start.5
  1.4 0.0 copy-start.6
  1.4 0.0 copy-start.7
  1.4 40.9 %forward.2 = (bf16[6,1024,512]{2,1,0:T(8,128)(2,1)}, bf16[6,1024,512]{2,1,0:T(8,128)(2,1)}, bf16[1024,768]{1,0:T(8,128)(2,1)}, f32[1024,768]{1,0:T(8,128)}, f32[...) custom-call(s32[1]{0:T(128)S(6)} %copy.44.refs_0_, ...), custom_call_target="tpu_custom_call" | custom-call | tf_op jit(solution)/shard_map/forward/pallas_call | solution.py:794
  42.9 0.0 copy-done
  42.9 0.0 copy-done.1
  42.9 0.0 copy-done.2
  42.9 0.0 copy-done.3
  42.9 0.0 copy-done.4
  42.9 0.0 copy-done.5
  42.9 0.0 copy-done.6
  42.9 0.0 copy-done.7
  42.9 113.9 %conditional.1 = ((f32[768,3072]{1,0:T(8,128)}, f32[3072,768]{1,0:T(8,128)}, f32[128,8,768]{2,1,0:T(8,128)}, f32[128,8,768]{2,1,0:T(8,128)}, f32[6,128]{1,0:T(8,...) conditional(s32[]{:T(128)} %bitcast, (s32[1]{0:T(128)}, ...), branch_computations={%region_0.0_spmd.clone, %region_1.0_spmd.clone} | conditional | bytes 8 | solution.py:1000
  43.2 100.0 %backward.3 = (bf16[6,6144,128]{2,1,0:T(8,128)(2,1)}, bf16[1024,768]{1,0:T(8,128)(2,1)}, f32[64,128]{1,0:T(8,128)}) custom-call(s32[1]{0:T(128)} %get-tuple-element.187.refs_0_.count_ref, s32[8]{0:T(128)S(1)} %get-tuple-element.188.refs_1_.length_ref, f32[768]{0:T(1024)S(1)} %get-tuple-element.189.refs_2_, f32[24,768]{1,0:T(8,128)S(1)} %get-tuple-element.190.refs_3_, ...), custom_call_target="tpu_custom_call" | custom-call | tf_op jit(solution)/shard_map/cond/branch_1_fun/backward/pallas_call | solution.py:855
  143.2 13.7 %output.3 = (f32[768,3072]{1,0:T(8,128)}, f32[3072,768]{1,0:T(8,128)}, f32[128,8,768]{2,1,0:T(8,128)}, f32[128,8,768]{2,1,0:T(8,128)}, f32[6,128]{1,0:T(8,128)},...) custom-call(s32[1]{0:T(128)} %get-tuple-element.187.refs_0_.count_ref, ...), custom_call_target="tpu_custom_call" | custom-call | tf_op jit(solution)/shard_map/cond/branch_1_fun/output/pallas_call | solution.py:947
Async XLA Ops:
  1.3 41.6 %copy-start = (bf16[4,256,512]{2,1,0:T(8,128)(2,1)S(1)}, bf16[4,256,512]{2,1,0:T(8,128)(2,1)}, u32[]{:S(2)}) copy-start(bf16[4,256,512]{2,1,0:T(8,128)(2,1)} %constant.7.clone.refs_12_) | copy-start | bytes 3145732
  1.3 41.6 %copy-start.1 = (f32[768]{0:T(1024)S(1)}, f32[768]{0:T(1024)}, u32[]{:S(2)}) copy-start(f32[768]{0:T(1024)} %refs_2_.1) | copy-start | bytes 9220
  1.3 41.6 %copy-start.2 = (f32[3072]{0:T(1024)S(1)}, f32[3072]{0:T(1024)}, u32[]{:S(2)}) copy-start(f32[3072]{0:T(1024)} %refs_7_.1) | copy-start | bytes 36868
  1.3 41.6 %copy-start.3 = (s32[8]{0:T(128)S(1)}, s32[8]{0:T(128)}, u32[]{:S(2)}) copy-start(s32[8]{0:T(128)} %refs_1_.1) | copy-start | bytes 100
  1.3 41.6 %copy-start.4 = (f32[768]{0:T(1024)S(1)}, f32[768]{0:T(1024)}, u32[]{:S(2)}) copy-start(f32[768]{0:T(1024)} %refs_3_.1) | copy-start | bytes 9220
  1.3 41.6 %copy-start.5 = (f32[768]{0:T(1024)S(1)}, f32[768]{0:T(1024)}, u32[]{:S(2)}) copy-start(f32[768]{0:T(1024)} %refs_4_.1) | copy-start | bytes 9220
  1.4 41.6 %copy-start.6 = (f32[768]{0:T(1024)S(1)}, f32[768]{0:T(1024)}, u32[]{:S(2)}) copy-start(f32[768]{0:T(1024)} %refs_5_.1) | copy-start | bytes 9220
  1.4 41.6 %copy-start.7 = (f32[768]{0:T(1024)S(1)}, f32[768]{0:T(1024)}, u32[]{:S(2)}) copy-start(f32[768]{0:T(1024)} %refs_6_.1) | copy-start | bytes 9220
where the time goes:
time: 158 us; the launch traced here: 157 us
  Pallas kernels  155 us (98%)
  between operations  2.24 us (1%)
    pallas_call x1, Pallas kernels, run_backward(): pl.pallas_call(functools.partial(backward_kernel, (sizes, far_slots, slot...  100 us
    pallas_call x1, Pallas kernels, run_forward(): pl.pallas_call(functools.partial(forward_kernel, (sizes, far_slots, slots...  40.9 us
    pallas_call x1, Pallas kernels, rest_of_layer(): pl.pallas_call(functools.partial(output_kernel, slots, cuts, places), nam...  13.7 us

commit v1 on v0

--- a/solution.py
+++ b/solution.py
@@ -267,7 +267,8 @@
         load.wait()
 
     batch = group * rows
-    span = features
+    folds = 2 if wide % (2 * features) == 0 else 1
+    span = folds * features
     count = slots // group
     near_groups = (slots - far_slots) // group
 
@@ -307,17 +308,14 @@
             pl.when(i < near_groups)(lambda: mixing(slot0, False))
         br_v[...] = jnp.dot(uv[...], hc_v[...], preferred_element_type=F32)
 
-        def norm_one(k, _):
+        for k in range(group):
             here = pl.ds(aligned(base + k * rows, rows), rows)
-            mixed = (br_v[pl.ds(aligned(k * rows, rows), rows), :] * scale).astype(BF16).astype(F32)
+            mixed = (br_v[k * rows : (k + 1) * rows, :] * scale).astype(BF16).astype(F32)
             live = live_rows(slen_s, slot0 + k, first, rows)
             total = jnp.where(live, x_v[:, perm_s[slot0 + k], :], 0.0) + mixed
             sum_v[here, :] = total
             hat, _ = normalize(total)
             nrm_v[here, :] = (hat * gain_one() + shift_one()).astype(BF16)
-            return 0
-
-        lax.fori_loop(0, group, norm_one, 0)
 
         @pl.when(i == 0)
         def _():
@@ -327,7 +325,8 @@
 
         def expand(n, _):
             cut = pl.ds(aligned(n * span, span), span)
-            hidden = jnp.dot(nrm_v[place, :], wi_v[:, cut], preferred_element_type=F32) + vec_ref[pl.ds(5 + n, 1), :]
+            bias = [vec_ref[pl.ds(5 + folds * n + i, 1), :] for i in range(folds)]
+            hidden = jnp.dot(nrm_v[place, :], wi_v[:, cut], preferred_element_type=F32) + jnp.concatenate(bias, axis=1)
             gate = 0.5 + 0.5 * lax.erf(hidden * math.sqrt(0.5))
             slope = gate + hidden * (jnp.exp(hidden * hidden * -0.5) * (1.0 / math.sqrt(2.0 * math.pi)))
             act_v[place, cut] = (hidden * gate).astype(BF16)

time: 158 us -> 156 us (0.987)
  Pallas kernels: 155 us -> 153 us
    pallas_call x1, Pallas kernels: 40.9 us -> 39 us  [run_forward(): pl.pallas_call(functools.partial(forward_kernel, (sizes, far_slots, slots...]
where the time goes in v1:
time: 156 us; the launch traced here: 155 us
  Pallas kernels  153 us (98%)
  between operations  2.24 us (1%)
    pallas_call x1, Pallas kernels, run_backward(): pl.pallas_call(functools.partial(backward_kernel, (sizes, far_slots, slot...  100 us
    pallas_call x1, Pallas kernels, run_forward(): pl.pallas_call(functools.partial(forward_kernel, (sizes, far_slots, slots...  39 us
    pallas_call x1, Pallas kernels, rest_of_layer(): pl.pallas_call(functools.partial(output_kernel, slots, cuts, places), nam...  13.7 us

profile of v1, /device:TPU:0, one launch (start us, length us, event | category | flops | bytes accessed | tf_op | source)
XLA Modules:
  0.0 155.2 jit_solution(15971051922457529224)
XLA Ops:
  1.3 0.0 copy-start
  1.3 0.0 copy-start.1
  1.3 0.0 copy-start.2
  1.3 0.0 copy-start.3
  1.3 0.0 copy-start.4
  1.3 0.0 copy-start.5
  1.4 0.0 copy-start.6
  1.4 0.0 copy-start.7
  1.4 39.0 %forward.2 = (bf16[6,1024,512]{2,1,0:T(8,128)(2,1)}, bf16[6,1024,512]{2,1,0:T(8,128)(2,1)}, bf16[1024,768]{1,0:T(8,128)(2,1)}, f32[1024,768]{1,0:T(8,128)}, f32[...) custom-call(s32[1]{0:T(128)S(6)} %copy.44.refs_0_, ...), custom_call_target="tpu_custom_call" | custom-call | tf_op jit(solution)/shard_map/forward/pallas_call | solution.py:793
  41.0 0.0 copy-done
  41.0 0.0 copy-done.1
  41.0 0.0 copy-done.2
  41.0 0.0 copy-done.3
  41.0 0.0 copy-done.4
  41.0 0.0 copy-done.5
  41.1 0.0 copy-done.6
  41.1 0.0 copy-done.7
  41.1 113.9 %conditional.1 = ((f32[768,3072]{1,0:T(8,128)}, f32[3072,768]{1,0:T(8,128)}, f32[128,8,768]{2,1,0:T(8,128)}, f32[128,8,768]{2,1,0:T(8,128)}, f32[6,128]{1,0:T(8,...) conditional(s32[]{:T(128)} %bitcast, (s32[1]{0:T(128)}, ...), branch_computations={%region_0.0_spmd.clone, %region_1.0_spmd.clone} | conditional | bytes 8 | solution.py:999
  41.3 100.0 %backward.3 = (bf16[6,6144,128]{2,1,0:T(8,128)(2,1)}, bf16[1024,768]{1,0:T(8,128)(2,1)}, f32[64,128]{1,0:T(8,128)}) custom-call(s32[1]{0:T(128)} %get-tuple-element.187.refs_0_.count_ref, s32[8]{0:T(128)S(1)} %get-tuple-element.188.refs_1_.length_ref, f32[768]{0:T(1024)S(1)} %get-tuple-element.189.refs_2_, f32[24,768]{1,0:T(8,128)S(1)} %get-tuple-element.190.refs_3_, ...), custom_call_target="tpu_custom_call" | custom-call | tf_op jit(solution)/shard_map/cond/branch_1_fun/backward/pallas_call | solution.py:854
  141.3 13.7 %output.3 = (f32[768,3072]{1,0:T(8,128)}, f32[3072,768]{1,0:T(8,128)}, f32[128,8,768]{2,1,0:T(8,128)}, f32[128,8,768]{2,1,0:T(8,128)}, f32[6,128]{1,0:T(8,128)},...) custom-call(s32[1]{0:T(128)} %get-tuple-element.187.refs_0_.count_ref, ...), custom_call_target="tpu_custom_call" | custom-call | tf_op jit(solution)/shard_map/cond/branch_1_fun/output/pallas_call | solution.py:946
Async XLA Ops:
  1.3 39.7 %copy-start = (bf16[4,256,512]{2,1,0:T(8,128)(2,1)S(1)}, bf16[4,256,512]{2,1,0:T(8,128)(2,1)}, u32[]{:S(2)}) copy-start(bf16[4,256,512]{2,1,0:T(8,128)(2,1)} %constant.7.clone.refs_12_) | copy-start | bytes 3145732
  1.3 39.7 %copy-start.1 = (f32[768]{0:T(1024)S(1)}, f32[768]{0:T(1024)}, u32[]{:S(2)}) copy-start(f32[768]{0:T(1024)} %refs_2_.1) | copy-start | bytes 9220
  1.3 39.7 %copy-start.2 = (f32[3072]{0:T(1024)S(1)}, f32[3072]{0:T(1024)}, u32[]{:S(2)}) copy-start(f32[3072]{0:T(1024)} %refs_7_.1) | copy-start | bytes 36868
  1.3 39.7 %copy-start.3 = (s32[8]{0:T(128)S(1)}, s32[8]{0:T(128)}, u32[]{:S(2)}) copy-start(s32[8]{0:T(128)} %refs_1_.1) | copy-start | bytes 100
  1.3 39.7 %copy-start.4 = (f32[768]{0:T(1024)S(1)}, f32[768]{0:T(1024)}, u32[]{:S(2)}) copy-start(f32[768]{0:T(1024)} %refs_3_.1) | copy-start | bytes 9220
  1.3 39.7 %copy-start.5 = (f32[768]{0:T(1024)S(1)}, f32[768]{0:T(1024)}, u32[]{:S(2)}) copy-start(f32[768]{0:T(1024)} %refs_4_.1) | copy-start | bytes 9220
  1.4 39.7 %copy-start.6 = (f32[768]{0:T(1024)S(1)}, f32[768]{0:T(1024)}, u32[]{:S(2)}) copy-start(f32[768]{0:T(1024)} %refs_5_.1) | copy-start | bytes 9220
  1.4 39.7 %copy-start.7 = (f32[768]{0:T(1024)S(1)}, f32[768]{0:T(1024)}, u32[]{:S(2)}) copy-start(f32[768]{0:T(1024)} %refs_6_.1) | copy-start | bytes 9220
